TPU v7x, 256 devices: a whole 4x4x8 slice. The times are simulated.
256 devices in a mesh: member: 4 (over y), band: 64 (over x, z, core).
Axes of the slice: x: 4, y: 4, z: 8, core: 2. Of those that a mesh axis runs over, the one named last changes fastest.
Arguments:
- predicted_states: bfloat16 [16, 100, 128, 1440], P('member', None, 'band'), may hold values from -6 to 6
- observed_truth: bfloat16 [100, 128, 1440], P(None, 'band', 'member'), may hold values from -6 to 6
- height_penalty_factor: float32 [100], replicated, may hold values from 0.5 to 5
Outputs:
- member_grad: bfloat16 [16, 100, 128, 1440], P('member', None, 'band')
- variable_loss: float32 [100], replicated
All inputs are finite; a program needn't handle non-finite values.
Results may differ from a plain program's by a relative error of at most 0.0055.
Values may be sent and summed in bfloat16 or wider, within the bound.
A program may use at most 64 MiB of HBM per device.

v0:
```python
import math

import jax
import jax.numpy as jnp
from jax import lax
from jax.sharding import PartitionSpec as P

alpha_fair = 0.95


def row_areas(parallel_band_sum):
    positions = jnp.arange(parallel_band_sum, dtype=jnp.float32)
    latitude = 0.5 * math.pi - math.pi * (positions + 0.5) / parallel_band_sum
    cosines = jnp.cos(latitude)
    return cosines / jnp.mean(cosines)


def add_pairs(carry, participant_private_map, others):
    sign_sum, abs_sum = carry
    for other in range(others.shape[0]):
        differ = participant_private_map - others[other].astype(jnp.float32)
        sign_sum = sign_sum + jnp.sign(differ)
        abs_sum = abs_sum + jnp.abs(differ)
    return (sign_sum, abs_sum)


def finish(
    participant_private_map, observed, sign_sum, abs_sum, weights, local_area, ensemble_collection
):
    fair = 1.0 - (1.0 - alpha_fair) / ensemble_collection
    scale = weights[None, :, None, None] * local_area[None, None, :, None]
    gradient = scale * (
        jnp.sign(participant_private_map - observed[None]) / ensemble_collection
        - fair * sign_sum / (ensemble_collection * (ensemble_collection - 1))
    )
    terms = local_area[None, None, :, None] * (
        jnp.abs(participant_private_map - observed[None]) / ensemble_collection
        - fair * abs_sum / (2 * ensemble_collection * (ensemble_collection - 1))
    )
    return (gradient.astype(jnp.bfloat16), jnp.sum(terms, axis=(0, 2, 3)))


def on_device(predicted_states, observed_truth, height_penalty_factor):
    bands_each_device = predicted_states.shape[2]
    parallel_band_sum = bands_each_device * lax.axis_size("band")
    ensemble_collection = predicted_states.shape[0] * lax.axis_size("member")
    mesh_cells = parallel_band_sum * predicted_states.shape[3]
    areas = row_areas(parallel_band_sum)
    local_area = lax.dynamic_slice_in_dim(
        areas, lax.axis_index("band") * bands_each_device, bands_each_device
    )
    observed = lax.all_gather(observed_truth, "member", axis=2, tiled=True)
    participant_private_map = predicted_states.astype(jnp.float32)
    blank_buffer = jnp.zeros(participant_private_map.shape, jnp.float32)
    sign_sum, abs_sum = add_pairs(
        (blank_buffer, blank_buffer),
        participant_private_map,
        lax.all_gather(predicted_states, "member", axis=0, tiled=True),
    )
    member_grad, partial_value = finish(
        participant_private_map,
        observed.astype(jnp.float32),
        sign_sum,
        abs_sum,
        height_penalty_factor,
        local_area,
        ensemble_collection,
    )
    accumulated_sums = lax.psum(partial_value, ("member", "band"))
    variable_loss = height_penalty_factor * accumulated_sums / mesh_cells
    return (member_grad, variable_loss)


def solution(mesh):
    in_specs = (P("member", None, "band", None), P(None, "band", "member"), P())
    out_specs = (P("member", None, "band", None), P())
    return jax.shard_map(
        on_device, mesh=mesh, in_specs=in_specs, out_specs=out_specs, check_vma=False
    )
```

profile of v0, /device:TPU:1, one launch (start us, length us, event | category | flops | bytes accessed | tf_op | source)
XLA Modules:
  0.0 353.4 jit_solution(17056933182352473311)
XLA Ops:
  7.2 0.0 all-gather.2.cloned.1.call-start
  7.2 0.7 all-gather.2.cloned.1.call-update
  7.9 1.1 copy.7
  9.0 13.2 %all_gather.6 = bf16[100,2,1440]{0,1,2:T(2,128)(2,1)S(1)} all-gather(bf16[100,2,360]{0,1,2:T(2,128)(2,1)S(1)} %copy.7), channel_id=1, replica_groups=mesh['member'=4,'band'=64] {'member'}, dimensions={2}, use_global_device_ids=true | all-gather | bytes 720000 | tf_op jit(solution)/shard_map/all_gather | solution.py:52
  22.2 1.8 copy.8
  24.1 1.4 convert_element_type.42
  25.5 0.7 fusion.90
  26.9 0.1 dynamic_slice.3
  27.0 0.1 broadcast_multiply_fusion
  27.1 0.0 copy-start
  27.1 84.5 %all-gather.2.cloned.1.call-done = bf16[16,100,2,1440]{3,2,1,0:T(2,128)(2,1)} async-done(((bf16[4,100,2,1440]{3,2,1,0:T(2,128)(2,1)}), bf16[16,100,2,1440]{3,2,1,0:T(2,128)(2,1)}) %all-gather.2.cloned.1.call-update) | async-done | bytes 9216016 | tf_op jit(solution)/shard_map/all_gather | solution.py:58
  111.5 10.6 %fusion.89 = (f32[100,2,1440]{2,1,0:T(2,128)S(1)}, f32[100,2,1440]{2,1,0:T(2,128)S(1)}, f32[100,2,1440]{2,1,0:T(2,128)S(1)}, f32[100,2,1440]{2,1,0:T(2,128)S(1)}...) fusion(bf16[16,100,2,1440]{3,2,1,0:T(2,128)(2,1)} %all-gather.2, ...), kind=kLoop, calls=%fused_computation.122 | loop fusion | flops 4608000 | bytes 27648000 | tf_op jit(solution)/shard_map/sub | solution.py:21
  122.3 0.9 copy-done.1
  123.2 0.4 copy-done.2
  123.6 0.4 copy-done.3
  124.0 0.4 copy-done.4
  124.3 0.4 copy-done.5
  124.7 0.4 copy-done.6
  125.1 0.3 copy-done.7
  125.5 0.4 copy-done.8
  125.8 0.4 copy-done.9
  126.3 0.3 copy-done.10
  126.6 0.4 copy-done.11
  127.0 0.4 copy-done.12
  127.4 0.3 copy-done.13
  127.7 0.3 copy-done.14
  128.0 0.5 copy-done.15
  128.5 0.3 copy-done.16
  128.8 37.5 %fusion.73 = f32[100]{0:T(128)S(1)} fusion(bf16[4,100,2,1440]{3,2,1,0:T(2,128)(2,1)S(1)} %copy-done, f32[2]{0:T(128)S(1)} %dynamic_slice.3, f32[100,2,1440]{2,1,0:T(2,128)S(1)} %get-tuple-element.3, f32[100,2,1440]{2,1,0:T(2,128)S(1)} %get-tuple-element.4, f32[100,2,1440]{2,1,0:T(2,128)S(1)} %get-tuple-element.5, f32[100,2,1440]{2,1,0:T(2,128)S(1)} %get-tuple-element.6, ...), kind=kLoop, calls=%fused_computation.90 | loop fusion | flops 63359900 | bytes 21888408 | tf_op jit(solution)/shard_map/reduce_sum | solution.py:40
  166.4 76.6 %psum.7 = f32[100]{0:T(128)S(1)} all-reduce(f32[100]{0:T(128)S(1)} %fusion.73), channel_id=1, replica_groups=mesh['member'=4,'band'=64] {'member','band'}, use_global_device_ids=true, to_apply=%region_2.0 | all-reduce | flops 100 | bytes 800 | tf_op jit(solution)/shard_map/psum | solution.py:69
  243.0 0.5 multiply_multiply_fusion
  243.5 103.0 %fusion.70 = bf16[4,100,2,1440]{3,2,1,0:T(2,128)(2,1)} fusion(bf16[4,100,2,1440]{3,2,1,0:T(2,128)(2,1)S(1)} %copy-done, f32[100,2,1440]{2,1,0:T(2,128)} %copy-done.2, f32[100,2,1440]{2,1,0:T(2,128)} %copy-done.3, f32[100,2,1440]{2,1,0:T(2,128)} %copy-done.4, f32[100,2,1440]{2,1,0:T(2,128)} %copy-done.5, f32[100,2,1440]{2,1,0:T(2,128)} %copy-done.6, ...), kind=kLoop, calls=%fused_computation.87 | loop fusion | flops 63360000 | bytes 24192800 | tf_op jit(solution)/shard_map/convert_element_type | solution.py:40
  (22 shorter events, 0.1 us)
Async XLA Ops:
  7.2 19.8 %copy-start.18 = (f32[100]{0:T(128)S(1)}, f32[100]{0:T(128)}, u32[]{:S(2)}) copy-start(f32[100]{0:T(128)} %param.5) | copy-start | bytes 1204
  7.2 104.4 %all-gather.2.cloned.1.call-start = ((), (), s32[]{:S(2)}) async-start(), calls=%async_computation | async-start | bytes 12288000 | tf_op jit(solution)/shard_map/all_gather | solution.py:58
  27.1 101.8 %copy-start = (bf16[4,100,2,1440]{3,2,1,0:T(2,128)(2,1)S(1)}, bf16[4,100,2,1440]{3,2,1,0:T(2,128)(2,1)}, u32[]{:S(2)}) copy-start(bf16[4,100,2,1440]{3,2,1,0:T(2,128)(2,1)} %param.3) | copy-start | bytes 6912004
  111.5 17.3 %copy-start.17 = (f32[100,2,1440]{2,1,0:T(2,128)S(1)}, f32[100,2,1440]{2,1,0:T(2,128)}, u32[]{:S(2)}) copy-start(f32[100,2,1440]{2,1,0:T(2,128)} %convert_element_type.42) | copy-start | bytes 3456004
  122.1 1.0 copy-start.1
  122.1 1.4 copy-start.2
  122.2 1.8 copy-start.3
  122.2 2.1 copy-start.4
  122.2 2.5 copy-start.5
  122.2 2.9 copy-start.6
  122.2 3.3 copy-start.7
  122.2 3.6 %copy-start.8 = (f32[100,2,1440]{2,1,0:T(2,128)}, f32[100,2,1440]{2,1,0:T(2,128)S(1)}, u32[]{:S(2)}) copy-start(f32[100,2,1440]{2,1,0:T(2,128)S(1)} %get-tuple-element.9) | copy-start | bytes 3456004
  122.2 4.1 %copy-start.9 = (f32[100,2,1440]{2,1,0:T(2,128)}, f32[100,2,1440]{2,1,0:T(2,128)S(1)}, u32[]{:S(2)}) copy-start(f32[100,2,1440]{2,1,0:T(2,128)S(1)} %get-tuple-element.10) | copy-start | bytes 3456004
  122.2 4.3 %copy-start.10 = (f32[100,2,1440]{2,1,0:T(2,128)}, f32[100,2,1440]{2,1,0:T(2,128)S(1)}, u32[]{:S(2)}) copy-start(f32[100,2,1440]{2,1,0:T(2,128)S(1)} %get-tuple-element.11) | copy-start | bytes 3456004
  122.2 4.8 %copy-start.11 = (f32[100,2,1440]{2,1,0:T(2,128)}, f32[100,2,1440]{2,1,0:T(2,128)S(1)}, u32[]{:S(2)}) copy-start(f32[100,2,1440]{2,1,0:T(2,128)S(1)} %get-tuple-element.12) | copy-start | bytes 3456004
  122.2 5.1 %copy-start.12 = (f32[100,2,1440]{2,1,0:T(2,128)}, f32[100,2,1440]{2,1,0:T(2,128)S(1)}, u32[]{:S(2)}) copy-start(f32[100,2,1440]{2,1,0:T(2,128)S(1)} %get-tuple-element.13) | copy-start | bytes 3456004
  122.3 5.4 %copy-start.13 = (f32[100,2,1440]{2,1,0:T(2,128)}, f32[100,2,1440]{2,1,0:T(2,128)S(1)}, u32[]{:S(2)}) copy-start(f32[100,2,1440]{2,1,0:T(2,128)S(1)} %get-tuple-element.14) | copy-start | bytes 3456004
  122.3 5.8 %copy-start.14 = (f32[100,2,1440]{2,1,0:T(2,128)}, f32[100,2,1440]{2,1,0:T(2,128)S(1)}, u32[]{:S(2)}) copy-start(f32[100,2,1440]{2,1,0:T(2,128)S(1)} %get-tuple-element.15) | copy-start | bytes 3456004
  122.3 6.2 %copy-start.15 = (f32[100,2,1440]{2,1,0:T(2,128)}, f32[100,2,1440]{2,1,0:T(2,128)S(1)}, u32[]{:S(2)}) copy-start(f32[100,2,1440]{2,1,0:T(2,128)S(1)} %get-tuple-element.16) | copy-start | bytes 3456004
  122.3 6.5 %copy-start.16 = (f32[100,2,1440]{2,1,0:T(2,128)}, f32[100,2,1440]{2,1,0:T(2,128)S(1)}, u32[]{:S(2)}) copy-start(f32[100,2,1440]{2,1,0:T(2,128)S(1)} %get-tuple-element.17) | copy-start | bytes 3456004
Sparse Core Ops, SparseCore 0:
  9.8 101.6 all-gather.1
where the time goes:
time: 354 us; the launch traced here: 353 us
  other arithmetic  154 us (44%)
  blocking collectives  89.9 us (25%)
  waiting for transfers between devices  85.1 us (24%)
  between operations  14.9 us (4%)
  local copies, waits for them, and re-layouts  9.57 us (3%)
    convert_element_type x1, other arithmetic, finish(): return (gradient.astype(jnp.bfloat16), jnp.sum(terms, axis=(0, 2, 3)))  103 us
    all_gather x1, waiting for transfers between devices, on_device(): lax.all_gather(predicted_states, 'member', axis=0, tiled=True)  84.5 us
    psum x1, blocking collectives, on_device(): accumulated_sums = lax.psum(partial_value, ('member', 'band'))  76.6 us
    reduce_sum x1, other arithmetic, finish(): return (gradient.astype(jnp.bfloat16), jnp.sum(terms, axis=(0, 2, 3)))  37.5 us
    all_gather x1, blocking collectives, on_device(): observed = lax.all_gather(observed_truth, 'member', axis=2, tiled=True)  13.2 us
    sub x1, other arithmetic, add_pairs(): differ = participant_private_map - others[other].astype(jnp.float32)  10.6 us
    unnamed x39, local copies, waits for them, and re-layouts  7.66 us
  transfers between devices with their start and end apart: 1, of which 1 were waited for; matrix products, arithmetic and copies ran while one was open for 1% of the time, Pallas kernels for 0%

commit v1 on v0

v1 whole, which is shorter than its diff:
```python
import functools
import math

import jax
import jax.numpy as jnp
import numpy as np
from jax import lax
from jax.experimental import pallas as pl
from jax.experimental.pallas import tpu as pltpu
from jax.sharding import PartitionSpec as P

MESH = pl.DeviceIdType.MESH
ALPHA_FAIR = 0.95
UP = 2.0**120
STEP = 2.0**-13
HALVES = ((0, 1024), (1024, 416))
Z, CORES = 8, 2


def mean_cosine(rows):
    positions = np.arange(rows, dtype=np.float64)
    return float(np.mean(np.cos(0.5 * math.pi - math.pi * (positions + 0.5) / rows)))


def rank_points(members, truth, truth32, weighted, member_value, put):
    count = len(members)
    fair = 1.0 - (1.0 - ALPHA_FAIR) / count
    low, high = jnp.bfloat16(-STEP), jnp.bfloat16(STEP)
    up = [m * jnp.bfloat16(UP) for m in members]
    truth_up = truth * jnp.bfloat16(UP)
    signs = [None] * count
    for j in range(count):
        for k in range(j + 1, count):
            s = jnp.minimum(jnp.maximum(up[j] - up[k], low), high)
            signs[j] = s if signs[j] is None else signs[j] + s
            signs[k] = -s if signs[k] is None else signs[k] - s
    total = None
    for j in range(count):
        beside = jnp.minimum(jnp.maximum(up[j] - truth_up, low), high).astype(jnp.float32)
        grad = beside * (1.0 / STEP / count) - signs[j].astype(jnp.float32) * (
            fair / STEP / (count * (count - 1))
        )
        term = (member_value(j).astype(jnp.float32) - truth32) * grad
        total = term if total is None else total + term
        put(j, (weighted * grad).astype(jnp.bfloat16))
    return total


def kernel(sizes, x_ref, t_ref, w_ref, y_ref, loss_ref, xs, ts, tf, ys, area, part, near, far, ring, *sems):
    members, levels, rows, cells, groups, bands, chunks = sizes
    own, deep = levels // groups, levels // groups // chunks
    (x_send, x_recv, x_sem, t_send, t_recv, t_sem, y_send, y_recv, y_sem, l_send, l_recv) = sems
    me, band = lax.axis_index("member"), lax.axis_index("band")
    core, z, x = lax.rem(band, CORES), lax.rem(band // CORES, Z), band // (CORES * Z)
    xs_count = bands // (CORES * Z)
    nears, fars = xs_count * CORES, Z
    near_me = x * CORES + core

    def member_at(d):
        return {"member": lax.rem(me + d, groups)}

    def near_at(d):
        i = lax.rem(near_me + d, nears)
        return i, {"band": ((i // CORES) * Z + z) * CORES + lax.rem(i, CORES)}

    def far_at(d):
        i = lax.rem(z + d, fars)
        return i, {"band": (x * Z + i) * CORES + core}

    peers = [member_at(d) for d in range(1, groups)]
    peers += [near_at(d)[1] for d in range(1, nears)]
    peers += [far_at(d)[1] for d in range(1, fars)]
    barrier = pltpu.get_barrier_semaphore()
    for peer in peers:
        pl.semaphore_signal(barrier, inc=1, device_id=peer, device_id_type=MESH)
    pl.semaphore_wait(barrier, len(peers))

    def send_t(d):
        return pltpu.make_async_remote_copy(
            t_ref.at[pl.ds(own * lax.rem(me + d, groups), own)], ts.at[me],
            t_send.at[d - 1], t_recv.at[d - 1], device_id=member_at(d), device_id_type=MESH,
        )

    def send_x(d, c):
        return pltpu.make_async_remote_copy(
            x_ref.at[:, pl.ds(own * lax.rem(me + d, groups) + deep * c, deep)],
            xs.at[groups - d, :, pl.ds(deep * c, deep)],
            x_send.at[d - 1, c], x_recv.at[d - 1, c], device_id=member_at(d), device_id_type=MESH,
        )

    def send_y(d, c):
        return pltpu.make_async_remote_copy(
            ys.at[d, :, pl.ds(deep * c, deep)],
            y_ref.at[:, pl.ds(own * me + deep * c, deep)],
            y_send.at[d - 1, c], y_recv.at[d - 1, c], device_id=member_at(d), device_id_type=MESH,
        )

    order = (1, 3, 2)
    keep_t = pltpu.make_async_copy(t_ref.at[pl.ds(own * me, own)], ts.at[me], t_sem)
    keep_x = pltpu.make_async_copy(x_ref.at[:, pl.ds(own * me, own)], xs.at[0], x_sem)
    for d in order:
        send_t(d).start()
    for c in range(chunks):
        for d in order:
            send_x(d, c).start()
        if c == 0:
            keep_t.start()
            keep_x.start()

    lat = 0.5 * math.pi - (math.pi / (bands * rows)) * (
        (lax.broadcasted_iota(jnp.int32, (rows, cells), 0) + band * rows).astype(jnp.float32) + 0.5
    )
    area[...] = jnp.cos(lat) * (1.0 / mean_cosine(bands * rows))
    part[...] = jnp.zeros_like(part)
    lanes = lax.broadcasted_iota(jnp.int32, (8, 128), 1)

    keep_t.wait()
    keep_x.wait()
    for d in order:
        send_t(d).wait_recv()

    def widen(v, carry):
        tf[v] = jnp.concatenate([ts[p, v].astype(jnp.float32) for p in range(groups)], axis=-1)
        return carry

    lax.fori_loop(0, own, widen, 0)

    def level(v, carry):
        weight = w_ref[own * me + v]
        loss = None
        for start, size in HALVES:
            cut = pl.ds(start, size)
            truth32 = tf[v, :, cut]
            area_here = area[:, cut]

            def member_value(j):
                return xs[j // members, j % members, v, :, cut]

            def put(j, value):
                ys[j // members, j % members, v, :, cut] = value

            total = rank_points(
                [member_value(j) for j in range(groups * members)],
                truth32.astype(jnp.bfloat16), truth32, weight * area_here, member_value, put,
            )
            total = jnp.sum(total * area_here)
            loss = total if loss is None else loss + total
        loss = loss * weight * (1.0 / (bands * rows * cells))
        part[...] += jnp.where(lanes == own * me + v, loss, 0.0)
        return carry

    def chunk(c, carry):
        for d in order:
            send_x(d, c).wait_recv()
        lax.fori_loop(c * deep, (c + 1) * deep, level, 0)
        for d in order:
            send_y(d, c).start()
        return carry

    lax.fori_loop(0, chunks, chunk, 0)
    keep_y = pltpu.make_async_copy(ys.at[0], y_ref.at[:, pl.ds(own * me, own)], y_sem)
    keep_y.start()

    def exchange(slots, count, mine, at, base):
        slots[mine] = part[...]

        def copy(d):
            i, peer = at(d)
            return pltpu.make_async_remote_copy(
                part, slots.at[mine], l_send.at[base + d], l_recv.at[base + d], device_id=peer, device_id_type=MESH,
            )

        for d in range(1, count):
            copy(d).start()
        for d in range(1, count):
            copy(d).wait()
        total = slots[0]
        for i in range(1, count):
            total = total + slots[i]
        part[...] = total

    exchange(near, nears, near_me, near_at, 0)
    exchange(far, fars, z, far_at, nears)
    exchange(ring, groups, me, lambda d: (d, member_at(d)), nears + fars)
    loss_ref[...] = part[0, :levels]

    for d in order:
        send_t(d).wait_send()

    def drain(c, carry):
        for d in order:
            send_x(d, c).wait_send()
            send_y(d, c).wait()
        return carry

    lax.fori_loop(0, chunks, drain, 0)
    keep_y.wait()


def solution(mesh):
    groups, bands = mesh.shape["member"], mesh.shape["band"]
    chunks = 5

    def on_device(predicted_states, observed_truth, height_penalty_factor):
        members, levels, rows, cells = predicted_states.shape
        own = levels // groups
        sizes = (members, levels, rows, cells, groups, bands, chunks)
        nears, fars = bands // Z, Z
        dma = pltpu.SemaphoreType.DMA
        peers = nears + fars + groups
        return pl.pallas_call(
            functools.partial(kernel, sizes),
            out_shape=(
                jax.ShapeDtypeStruct(predicted_states.shape, jnp.bfloat16),
                jax.ShapeDtypeStruct((levels,), jnp.float32),
            ),
            in_specs=[pl.BlockSpec(memory_space=pltpu.HBM)] * 2 + [pl.BlockSpec(memory_space=pltpu.SMEM)],
            out_specs=(pl.BlockSpec(memory_space=pl.ANY), pl.BlockSpec(memory_space=pltpu.VMEM)),
            scratch_shapes=[
                pltpu.VMEM((groups, members, own, rows, cells), jnp.bfloat16),
                pltpu.VMEM((groups, own, rows, cells // groups), jnp.bfloat16),
                pltpu.VMEM((own, rows, cells), jnp.float32),
                pltpu.VMEM((groups, members, own, rows, cells), jnp.bfloat16),
                pltpu.VMEM((rows, cells), jnp.float32),
                pltpu.VMEM((8, 128), jnp.float32),
                pltpu.VMEM((nears, 8, 128), jnp.float32),
                pltpu.VMEM((fars, 8, 128), jnp.float32),
                pltpu.VMEM((groups, 8, 128), jnp.float32),
                dma((groups - 1, chunks)), dma((groups - 1, chunks)), dma,
                dma((groups - 1,)), dma((groups - 1,)), dma,
                dma((groups - 1, chunks)), dma((groups - 1, chunks)), dma,
                dma((peers,)), dma((peers,)),
            ],
            compiler_params=pltpu.CompilerParams(
                collective_id=0, has_side_effects=True, vmem_limit_bytes=56 * 2**20
            ),
        )(predicted_states, observed_truth, height_penalty_factor)

    in_specs = (P("member", None, "band", None), P(None, "band", "member"), P())
    out_specs = (P("member", None, "band", None), P())
    return jax.shard_map(on_device, mesh=mesh, in_specs=in_specs, out_specs=out_specs, check_vma=False)
```

time: 354 us -> 74.3 us (0.21)
  other arithmetic: 154 us -> 0 us
  blocking collectives: 89.9 us -> 0 us
  waiting for transfers between devices: 85.1 us -> 0 us
  Pallas kernels: 0 us -> 68.2 us
  between operations: 14.9 us -> 0.65 us
  local copies, waits for them, and re-layouts: 9.57 us -> 5.33 us
    convert_element_type x2 -> x0, other arithmetic: 104 us -> none  [the longest x1 103 us: finish(): return (gradient.astype(jnp.bfloat16), jnp.sum(terms, axis=(0, 2, 3)))]
    all_gather x1 -> x0, waiting for transfers between devices: 84.5 us -> none  [on_device(): lax.all_gather(predicted_states, 'member', axis=0, tiled=True)]
    psum x1 -> x0, blocking collectives: 76.6 us -> none  [on_device(): accumulated_sums = lax.psum(partial_value, ('member', 'band'))]
    pallas_call x0 -> x1, Pallas kernels: none -> 68.2 us  [on_device(): pl.pallas_call(functools.partial(kernel, sizes), out_shape=(jax.ShapeDtyp...]
    reduce_sum x2 -> x0, other arithmetic: 38.2 us -> none  [the longest x1 37.5 us: finish(): return (gradient.astype(jnp.bfloat16), jnp.sum(terms, axis=(0, 2, 3)))]
    all_gather x1 -> x0, blocking collectives: 13.2 us -> none  [on_device(): observed = lax.all_gather(observed_truth, 'member', axis=2, tiled=True)]
    sub x1 -> x0, other arithmetic: 10.6 us -> none  [add_pairs(): differ = participant_private_map - others[other].astype(jnp.float32)]
    unnamed x39 -> x4, local copies, waits for them, and re-layouts: 7.66 us -> 5.33 us
  transfers between devices with their start and end apart: 1 -> 0, of which waited for: 1 -> 0; matrix products, arithmetic and copies ran while one was open for 1% -> 0% of each run, Pallas kernels for 0% -> 0%
where the time goes in v1:
time: 74.3 us; the launch traced here: 74.2 us
  Pallas kernels  68.2 us (92%)
  local copies, waits for them, and re-layouts  5.33 us (7%)
    pallas_call x1, Pallas kernels, on_device(): pl.pallas_call(functools.partial(kernel, sizes), out_shape=(jax.ShapeDtyp...  68.2 us
    unnamed x4, local copies, waits for them, and re-layouts  5.33 us

profile of v1, /device:TPU:1, one launch (start us, length us, event | category | flops | bytes accessed | tf_op | source)
XLA Modules:
  0.0 74.2 jit_solution(15419297611445635873)
XLA Ops:
  0.6 68.2 %shard_map.50 = (bf16[4,100,2,1440]{3,2,1,0:T(2,128)(2,1)}, f32[100]{0:T(128)}) custom-call(bf16[4,100,2,1440]{3,2,1,0:T(2,128)(2,1)} %x_ref.1, bf16[100,2,360]{2,1,0:T(2,128)(2,1)} %t_ref.1, f32[100]{0:T(128)} %w_ref.1), custom_call_target="tpu_custom_call" | custom-call | tf_op jit(solution)/shard_map/pallas_call | solution.py:211
  68.8 0.0 copy-start
  68.8 4.8 %copy.7 = bf16[4,100,2,1440]{3,2,1,0:T(2,128)(2,1)} copy(bf16[4,100,2,1440]{3,2,1,0:T(2,128)(2,1)} %get-tuple-element.4) | data formatting | bytes 4608000
  73.7 0.0 copy-done
  73.7 0.5 copy.8
Async XLA Ops:
  68.8 4.8 %copy-start = (f32[100]{0:T(128)S(1)}, f32[100]{0:T(128)}, u32[]{:S(2)}) copy-start(f32[100]{0:T(128)} %get-tuple-element.5) | copy-start | bytes 1204

commit v2 on v1

--- a/solution.py
+++ b/solution.py
@@ -46,34 +46,63 @@
     return total
 
 
-def kernel(sizes, x_ref, t_ref, w_ref, y_ref, loss_ref, xs, ts, tf, ys, area, part, near, far, ring, *sems):
+def kernel(sizes, x_ref, t_ref, w_ref, y_ref, loss_ref, xs, ts, tf, ys, area, part, ring, near, far, ready, opened, *sems):
     members, levels, rows, cells, groups, bands, chunks = sizes
     own, deep = levels // groups, levels // groups // chunks
     (x_send, x_recv, x_sem, t_send, t_recv, t_sem, y_send, y_recv, y_sem, l_send, l_recv) = sems
     me, band = lax.axis_index("member"), lax.axis_index("band")
     core, z, x = lax.rem(band, CORES), lax.rem(band // CORES, Z), band // (CORES * Z)
-    xs_count = bands // (CORES * Z)
-    nears, fars = xs_count * CORES, Z
-    near_me = x * CORES + core
+    wide, tall = bands // (CORES * Z), Z
 
     def member_at(d):
         return {"member": lax.rem(me + d, groups)}
 
-    def near_at(d):
-        i = lax.rem(near_me + d, nears)
-        return i, {"band": ((i // CORES) * Z + z) * CORES + lax.rem(i, CORES)}
-
-    def far_at(d):
-        i = lax.rem(z + d, fars)
-        return i, {"band": (x * Z + i) * CORES + core}
-
-    peers = [member_at(d) for d in range(1, groups)]
-    peers += [near_at(d)[1] for d in range(1, nears)]
-    peers += [far_at(d)[1] for d in range(1, fars)]
+    def across(d):
+        return {"band": (lax.rem(x + d, wide) * Z + z) * CORES + core}
+
+    def around(d):
+        i = lax.rem(x * CORES + core + d, wide * CORES)
+        return {"band": ((i // CORES) * Z + z) * CORES + lax.rem(i, CORES)}
+
+    def along(d):
+        return {"band": (x * Z + lax.rem(z + d, tall)) * CORES + core}
+
+    partner = {"band": band + 1 - 2 * core}
+    head = (me == 0) & (core == 0)
+    heads = [across(d) for d in range(1, wide)] + [along(d) for d in range(1, tall)]
+
     barrier = pltpu.get_barrier_semaphore()
-    for peer in peers:
-        pl.semaphore_signal(barrier, inc=1, device_id=peer, device_id_type=MESH)
-    pl.semaphore_wait(barrier, len(peers))
+
+    def greet(sem, peer):
+        pl.semaphore_signal(sem, inc=1, device_id=peer, device_id_type=MESH)
+
+    for d in range(1, groups):
+
+        @pl.when(jnp.logical_not((lax.rem(me + d, groups) == 0) & (core == 0)))
+        def _():
+            greet(barrier, member_at(d))
+
+    @pl.when(jnp.logical_not((me == 0) & (core == 1)))
+    def _():
+        greet(barrier, partner)
+
+    @pl.when(jnp.logical_not(head))
+    def _():
+        pl.semaphore_wait(barrier, groups)
+
+        @pl.when(core == 0)
+        def _():
+            greet(ready, {"member": 0})
+
+        @pl.when(me == 0)
+        def _():
+            greet(ready, partner)
+
+    @pl.when(head)
+    def _():
+        pl.semaphore_wait(ready, groups)
+        for peer in heads:
+            greet(barrier, peer)
 
     def send_t(d):
         return pltpu.make_async_remote_copy(
@@ -139,17 +168,25 @@
             def put(j, value):
                 ys[j // members, j % members, v, :, cut] = value
 
-            total = rank_points(
+            block = rank_points(
                 [member_value(j) for j in range(groups * members)],
                 truth32.astype(jnp.bfloat16), truth32, weight * area_here, member_value, put,
             )
-            total = jnp.sum(total * area_here)
-            loss = total if loss is None else loss + total
+            block = jnp.sum(block * area_here)
+            loss = block if loss is None else loss + block
         loss = loss * weight * (1.0 / (bands * rows * cells))
         part[...] += jnp.where(lanes == own * me + v, loss, 0.0)
         return carry
 
     def chunk(c, carry):
+        @pl.when(head & (c == 2))
+        def _():
+            pl.semaphore_wait(barrier, len(heads))
+            for m in range(groups):
+                for other in range(CORES):
+                    if m + other:
+                        greet(opened, {"member": m, "band": band + other})
+
         for d in order:
             send_x(d, c).wait_recv()
         lax.fori_loop(c * deep, (c + 1) * deep, level, 0)
@@ -161,27 +198,32 @@
     keep_y = pltpu.make_async_copy(ys.at[0], y_ref.at[:, pl.ds(own * me, own)], y_sem)
     keep_y.start()
 
-    def exchange(slots, count, mine, at, base):
-        slots[mine] = part[...]
-
-        def copy(d):
-            i, peer = at(d)
-            return pltpu.make_async_remote_copy(
-                part, slots.at[mine], l_send.at[base + d], l_recv.at[base + d], device_id=peer, device_id_type=MESH,
-            )
-
-        for d in range(1, count):
-            copy(d).start()
-        for d in range(1, count):
-            copy(d).wait()
+    def move(src, dst, i, peer):
+        return pltpu.make_async_remote_copy(
+            src, dst, l_send.at[i], l_recv.at[i], device_id=peer, device_id_type=MESH
+        )
+
+    def add_up(slots, count):
         total = slots[0]
         for i in range(1, count):
             total = total + slots[i]
-        part[...] = total
-
-    exchange(near, nears, near_me, near_at, 0)
-    exchange(far, fars, z, far_at, nears)
-    exchange(ring, groups, me, lambda d: (d, member_at(d)), nears + fars)
+        return total
+
+    def exchange(slots, count, mine, at, base):
+        slots[mine] = part[...]
+        for d in range(1, count):
+            move(part, slots.at[mine], base + d - 1, at(d)).start()
+        for d in range(1, count):
+            move(part, slots.at[mine], base + d - 1, at(d)).wait()
+        part[...] = add_up(slots, count)
+
+    @pl.when(jnp.logical_not(head))
+    def _():
+        pl.semaphore_wait(opened, 1)
+
+    exchange(near, wide * CORES, x * CORES + core, around, 0)
+    exchange(far, tall, z, along, wide * CORES)
+    exchange(ring, groups, me, member_at, wide * CORES + tall)
     loss_ref[...] = part[0, :levels]
 
     for d in order:
@@ -205,13 +247,13 @@
         members, levels, rows, cells = predicted_states.shape
         own = levels // groups
         sizes = (members, levels, rows, cells, groups, bands, chunks)
-        nears, fars = bands // Z, Z
+        wide, tall = bands // (CORES * Z), Z
         dma = pltpu.SemaphoreType.DMA
-        peers = nears + fars + groups
+        peers = wide * CORES + tall + groups
         return pl.pallas_call(
             functools.partial(kernel, sizes),
             out_shape=(
-                jax.ShapeDtypeStruct(predicted_states.shape, jnp.bfloat16),
+                pltpu.VMEM(predicted_states.shape, jnp.bfloat16),
                 jax.ShapeDtypeStruct((levels,), jnp.float32),
             ),
             in_specs=[pl.BlockSpec(memory_space=pltpu.HBM)] * 2 + [pl.BlockSpec(memory_space=pltpu.SMEM)],
@@ -223,9 +265,10 @@
                 pltpu.VMEM((groups, members, own, rows, cells), jnp.bfloat16),
                 pltpu.VMEM((rows, cells), jnp.float32),
                 pltpu.VMEM((8, 128), jnp.float32),
-                pltpu.VMEM((nears, 8, 128), jnp.float32),
-                pltpu.VMEM((fars, 8, 128), jnp.float32),
                 pltpu.VMEM((groups, 8, 128), jnp.float32),
+                pltpu.VMEM((wide * CORES, 8, 128), jnp.float32),
+                pltpu.VMEM((tall, 8, 128), jnp.float32),
+                pltpu.SemaphoreType.REGULAR, pltpu.SemaphoreType.REGULAR,
                 dma((groups - 1, chunks)), dma((groups - 1, chunks)), dma,
                 dma((groups - 1,)), dma((groups - 1,)), dma,
                 dma((groups - 1, chunks)), dma((groups - 1, chunks)), dma,

time: 74.3 us -> 64.8 us (0.87)
  Pallas kernels: 68.2 us -> 61.4 us
  local copies, waits for them, and re-layouts: 5.33 us -> 1.96 us
    pallas_call x1, Pallas kernels: 68.2 us -> 61.4 us  [on_device(): pl.pallas_call(functools.partial(kernel, sizes), out_shape=(pltpu.VMEM(pr...]
    unnamed x4, local copies, waits for them, and re-layouts: 5.33 us -> 1.96 us
where the time goes in v2:
time: 64.8 us; the launch traced here: 64 us
  Pallas kernels  61.4 us (95%)
  local copies, waits for them, and re-layouts  1.96 us (3%)
  between operations  0.65 us (1%)
    pallas_call x1, Pallas kernels, on_device(): pl.pallas_call(functools.partial(kernel, sizes), out_shape=(pltpu.VMEM(pr...  61.4 us
    unnamed x4, local copies, waits for them, and re-layouts  1.96 us

profile of v2, /device:TPU:1, one launch (start us, length us, event | category | flops | bytes accessed | tf_op | source)
XLA Modules:
  0.0 64.0 jit_solution(9786189805696253403)
XLA Ops:
  0.6 61.4 %shard_map.50 = (bf16[4,100,2,1440]{3,2,1,0:T(2,128)(2,1)S(1)}, f32[100]{0:T(128)}) custom-call(bf16[4,100,2,1440]{3,2,1,0:T(2,128)(2,1)} %x_ref.1, bf16[100,2,360]{2,1,0:T(2,128)(2,1)} %t_ref.1, f32[100]{0:T(128)} %w_ref.1), custom_call_target="tpu_custom_call" | custom-call | tf_op jit(solution)/shard_map/pallas_call | solution.py:253
  62.1 0.0 copy-start
  62.1 1.4 %copy.7 = bf16[4,100,2,1440]{3,2,1,0:T(2,128)(2,1)} copy(bf16[4,100,2,1440]{3,2,1,0:T(2,128)(2,1)S(1)} %get-tuple-element.2) | data formatting | bytes 4608000
  63.5 0.0 copy-done
  63.5 0.5 copy.8
Async XLA Ops:
  62.1 1.5 %copy-start = (f32[100]{0:T(128)S(1)}, f32[100]{0:T(128)}, u32[]{:S(2)}) copy-start(f32[100]{0:T(128)} %get-tuple-element.7) | copy-start | bytes 1204

commit v3 on v2

--- a/solution.py
+++ b/solution.py
@@ -13,7 +13,9 @@
 ALPHA_FAIR = 0.95
 UP = 2.0**120
 STEP = 2.0**-13
-HALVES = ((0, 1024), (1024, 416))
+LANES = 128
+FRONT = 1024
+PIECES = 1
 Z, CORES = 8, 2
 
 
@@ -46,10 +48,18 @@
     return total
 
 
-def kernel(sizes, x_ref, t_ref, w_ref, y_ref, loss_ref, xs, ts, tf, ys, area, part, ring, near, far, ready, opened, *sems):
-    members, levels, rows, cells, groups, bands, chunks = sizes
+def kernel(
+    sizes, x_ref, t_ref, w_hbm, y_ref, loss_ref, xs, ts, tf, ys, area, part, ring, near, far, w_ref,
+    x_edge, xe_out, xe_in, ye_out, ye_in, y_edge, ready, opened, *sems,
+):
+    members, levels, rows, cells, groups, bands, chunks, early = sizes
     own, deep = levels // groups, levels // groups // chunks
-    (x_send, x_recv, x_sem, t_send, t_recv, t_sem, y_send, y_recv, y_sem, l_send, l_recv) = sems
+    (x_send, x_recv, x_sem, t_send, t_recv, t_sem, y_send, y_recv, y_sem, l_send, l_recv) = sems[:11]
+    (xe_send, xe_recv, xe_sem, ye_send, ye_recv, ye_sem, w_sem) = sems[11:]
+    whole = cells // LANES * LANES
+    edge = cells - whole
+    body, rim = pl.ds(0, whole), pl.ds(whole, edge)
+    everyone = groups * members
     me, band = lax.axis_index("member"), lax.axis_index("band")
     core, z, x = lax.rem(band, CORES), lax.rem(band // CORES, Z), band // (CORES * Z)
     wide, tall = bands // (CORES * Z), Z
@@ -71,6 +81,10 @@
     head = (me == 0) & (core == 0)
     heads = [across(d) for d in range(1, wide)] + [along(d) for d in range(1, tall)]
 
+    keep_w = pltpu.make_async_copy(w_hbm, w_ref, w_sem)
+    keep_w.start()
+    keep_xe = pltpu.make_async_copy(x_ref.at[:, :, :, rim], x_edge, xe_sem)
+    keep_xe.start()
     barrier = pltpu.get_barrier_semaphore()
 
     def greet(sem, peer):
@@ -112,7 +126,7 @@
 
     def send_x(d, c):
         return pltpu.make_async_remote_copy(
-            x_ref.at[:, pl.ds(own * lax.rem(me + d, groups) + deep * c, deep)],
+            x_ref.at[:, pl.ds(own * lax.rem(me + d, groups) + deep * c, deep), :, body],
             xs.at[groups - d, :, pl.ds(deep * c, deep)],
             x_send.at[d - 1, c], x_recv.at[d - 1, c], device_id=member_at(d), device_id_type=MESH,
         )
@@ -120,21 +134,57 @@
     def send_y(d, c):
         return pltpu.make_async_remote_copy(
             ys.at[d, :, pl.ds(deep * c, deep)],
-            y_ref.at[:, pl.ds(own * me + deep * c, deep)],
+            y_ref.at[:, pl.ds(own * me + deep * c, deep), :, body],
             y_send.at[d - 1, c], y_recv.at[d - 1, c], device_id=member_at(d), device_id_type=MESH,
+        )
+
+    def send_xe(d):
+        return pltpu.make_async_remote_copy(
+            xe_out.at[d], xe_in.at[groups - d], xe_send.at[d - 1], xe_recv.at[d - 1],
+            device_id=member_at(d), device_id_type=MESH,
+        )
+
+    def send_ye(d):
+        return pltpu.make_async_remote_copy(
+            ye_out.at[d], ye_in.at[groups - d], ye_send.at[d - 1], ye_recv.at[d - 1],
+            device_id=member_at(d), device_id_type=MESH,
         )
 
     order = (1, 3, 2)
     keep_t = pltpu.make_async_copy(t_ref.at[pl.ds(own * me, own)], ts.at[me], t_sem)
-    keep_x = pltpu.make_async_copy(x_ref.at[:, pl.ds(own * me, own)], xs.at[0], x_sem)
+    keep_x = pltpu.make_async_copy(x_ref.at[:, pl.ds(own * me, own), :, body], xs.at[0], x_sem)
     for d in order:
         send_t(d).start()
-    for c in range(chunks):
+    for c in range(early):
         for d in order:
             send_x(d, c).start()
-        if c == 0:
-            keep_t.start()
-            keep_x.start()
+    keep_t.start()
+    keep_x.start()
+
+    keep_xe.wait()
+
+    def pack(i, carry):
+        d, m = i // members, lax.rem(i, members)
+        first = own * lax.rem(me + d, groups)
+        row = [x_edge[m, first + v].astype(jnp.float32) for v in range(own)]
+        row = jnp.concatenate(row, axis=-1).astype(jnp.bfloat16)
+
+        @pl.when(d == 0)
+        def _():
+            xe_in[0, m] = row
+
+        @pl.when(d > 0)
+        def _():
+            xe_out[d, m] = row
+
+        return carry
+
+    lax.fori_loop(0, everyone, pack, 0)
+    for d in order:
+        send_xe(d).start()
+    for c in range(early, chunks):
+        for d in order:
+            send_x(d, c).start()
 
     lat = 0.5 * math.pi - (math.pi / (bands * rows)) * (
         (lax.broadcasted_iota(jnp.int32, (rows, cells), 0) + band * rows).astype(jnp.float32) + 0.5
@@ -143,6 +193,7 @@
     part[...] = jnp.zeros_like(part)
     lanes = lax.broadcasted_iota(jnp.int32, (8, 128), 1)
 
+    keep_w.wait()
     keep_t.wait()
     keep_x.wait()
     for d in order:
@@ -157,7 +208,7 @@
     def level(v, carry):
         weight = w_ref[own * me + v]
         loss = None
-        for start, size in HALVES:
+        for start, size in ((0, FRONT), (FRONT, whole - FRONT)):
             cut = pl.ds(start, size)
             truth32 = tf[v, :, cut]
             area_here = area[:, cut]
@@ -169,7 +220,7 @@
                 ys[j // members, j % members, v, :, cut] = value
 
             block = rank_points(
-                [member_value(j) for j in range(groups * members)],
+                [member_value(j) for j in range(everyone)],
                 truth32.astype(jnp.bfloat16), truth32, weight * area_here, member_value, put,
             )
             block = jnp.sum(block * area_here)
@@ -178,6 +229,35 @@
         part[...] += jnp.where(lanes == own * me + v, loss, 0.0)
         return carry
 
+    def edges():
+        for d in order:
+            send_xe(d).wait_recv()
+        truth32 = jnp.concatenate([tf[v, :, rim] for v in range(own)], axis=-1)
+        weights = [w_ref[own * me + v] for v in range(own)]
+        area_here = area[:, : own * edge]
+        wide_weight = jnp.concatenate([jnp.full((rows, edge), w, jnp.float32) for w in weights], axis=-1)
+
+        def member_value(j):
+            return xe_in[j // members, j % members]
+
+        def put(j, value):
+            if j < members:
+                ye_in[0, j] = value
+            else:
+                ye_out[j // members, j % members] = value
+
+        block = rank_points(
+            [member_value(j) for j in range(everyone)],
+            truth32.astype(jnp.bfloat16), truth32, wide_weight * area_here, member_value, put,
+        )
+        block = block * area_here * wide_weight * (1.0 / (bands * rows * cells))
+        loss = part[...]
+        for v in range(own):
+            loss = loss + jnp.where(lanes == own * me + v, jnp.sum(block[:, edge * v : edge * (v + 1)]), 0.0)
+        part[...] = loss
+        for d in order:
+            send_ye(d).start()
+
     def chunk(c, carry):
         @pl.when(head & (c == 2))
         def _():
@@ -192,10 +272,11 @@
         lax.fori_loop(c * deep, (c + 1) * deep, level, 0)
         for d in order:
             send_y(d, c).start()
+        pl.when(c == early - 1)(edges)
         return carry
 
     lax.fori_loop(0, chunks, chunk, 0)
-    keep_y = pltpu.make_async_copy(ys.at[0], y_ref.at[:, pl.ds(own * me, own)], y_sem)
+    keep_y = pltpu.make_async_copy(ys.at[0], y_ref.at[:, pl.ds(own * me, own), :, body], y_sem)
     keep_y.start()
 
     def move(src, dst, i, peer):
@@ -209,10 +290,12 @@
             total = total + slots[i]
         return total
 
-    def exchange(slots, count, mine, at, base):
+    def hand_out(slots, count, mine, at, base):
         slots[mine] = part[...]
         for d in range(1, count):
             move(part, slots.at[mine], base + d - 1, at(d)).start()
+
+    def take_in(slots, count, mine, at, base):
         for d in range(1, count):
             move(part, slots.at[mine], base + d - 1, at(d)).wait()
         part[...] = add_up(slots, count)
@@ -221,13 +304,35 @@
     def _():
         pl.semaphore_wait(opened, 1)
 
-    exchange(near, wide * CORES, x * CORES + core, around, 0)
-    exchange(far, tall, z, along, wide * CORES)
-    exchange(ring, groups, me, member_at, wide * CORES + tall)
+    by_x = (near, wide * CORES, x * CORES + core, around, 0)
+    by_z = (far, tall, z, along, wide * CORES)
+    by_y = (ring, groups, me, member_at, wide * CORES + tall)
+    hand_out(*by_x)
+    take_in(*by_x)
+    hand_out(*by_z)
+    take_in(*by_z)
+    hand_out(*by_y)
+
+    def unpack(i, carry):
+        d, m = i // members, lax.rem(i, members)
+        first = own * lax.rem(me + d, groups)
+        row = ye_in[d, m].astype(jnp.float32)
+        for v in range(own):
+            y_edge[m, first + v] = row[:, edge * v : edge * (v + 1)].astype(jnp.bfloat16)
+        return carry
+
+    for d in order:
+        send_ye(d).wait_recv()
+    lax.fori_loop(0, everyone, unpack, 0)
+    keep_ye = pltpu.make_async_copy(y_edge, y_ref.at[:, :, :, rim], ye_sem)
+    keep_ye.start()
+    take_in(*by_y)
     loss_ref[...] = part[0, :levels]
 
     for d in order:
         send_t(d).wait_send()
+        send_xe(d).wait_send()
+        send_ye(d).wait_send()
 
     def drain(c, carry):
         for d in order:
@@ -237,48 +342,84 @@
 
     lax.fori_loop(0, chunks, drain, 0)
     keep_y.wait()
+    keep_ye.wait()
+
+
+def settle(pieces, grad_ref, loss_ref, grad_out, loss_out, sems, loss_sem):
+    members, levels = grad_ref.shape[:2]
+    step = levels // pieces
+    copies = [pltpu.make_async_copy(loss_ref, loss_out, loss_sem)]
+    for m in range(members):
+        for i in range(pieces):
+            cut = pl.ds(i * step, step)
+            copies.append(pltpu.make_async_copy(grad_ref.at[m, cut], grad_out.at[m, cut], sems.at[m, i]))
+    for copy in copies:
+        copy.start()
+    for copy in copies:
+        copy.wait()
 
 
 def solution(mesh):
     groups, bands = mesh.shape["member"], mesh.shape["band"]
-    chunks = 5
+    chunks, early = 5, 2
 
     def on_device(predicted_states, observed_truth, height_penalty_factor):
         members, levels, rows, cells = predicted_states.shape
         own = levels // groups
-        sizes = (members, levels, rows, cells, groups, bands, chunks)
+        sizes = (members, levels, rows, cells, groups, bands, chunks, early)
+        whole = cells // LANES * LANES
+        packed = (groups, members, rows, own * (cells - whole))
         wide, tall = bands // (CORES * Z), Z
         dma = pltpu.SemaphoreType.DMA
         peers = wide * CORES + tall + groups
-        return pl.pallas_call(
+        grad, loss = pl.pallas_call(
             functools.partial(kernel, sizes),
             out_shape=(
                 pltpu.VMEM(predicted_states.shape, jnp.bfloat16),
-                jax.ShapeDtypeStruct((levels,), jnp.float32),
+                pltpu.VMEM((levels,), jnp.float32),
             ),
-            in_specs=[pl.BlockSpec(memory_space=pltpu.HBM)] * 2 + [pl.BlockSpec(memory_space=pltpu.SMEM)],
+            in_specs=[pl.BlockSpec(memory_space=pltpu.HBM)] * 2 + [pl.BlockSpec(memory_space=pltpu.HBM)],
             out_specs=(pl.BlockSpec(memory_space=pl.ANY), pl.BlockSpec(memory_space=pltpu.VMEM)),
             scratch_shapes=[
-                pltpu.VMEM((groups, members, own, rows, cells), jnp.bfloat16),
+                pltpu.VMEM((groups, members, own, rows, whole), jnp.bfloat16),
                 pltpu.VMEM((groups, own, rows, cells // groups), jnp.bfloat16),
                 pltpu.VMEM((own, rows, cells), jnp.float32),
-                pltpu.VMEM((groups, members, own, rows, cells), jnp.bfloat16),
+                pltpu.VMEM((groups, members, own, rows, whole), jnp.bfloat16),
                 pltpu.VMEM((rows, cells), jnp.float32),
                 pltpu.VMEM((8, 128), jnp.float32),
                 pltpu.VMEM((groups, 8, 128), jnp.float32),
                 pltpu.VMEM((wide * CORES, 8, 128), jnp.float32),
                 pltpu.VMEM((tall, 8, 128), jnp.float32),
+                pltpu.SMEM((levels,), jnp.float32),
+                pltpu.VMEM((members, levels, rows, cells - whole), jnp.bfloat16),
+                pltpu.VMEM(packed, jnp.bfloat16), pltpu.VMEM(packed, jnp.bfloat16),
+                pltpu.VMEM(packed, jnp.bfloat16), pltpu.VMEM(packed, jnp.bfloat16),
+                pltpu.VMEM((members, levels, rows, cells - whole), jnp.bfloat16),
                 pltpu.SemaphoreType.REGULAR, pltpu.SemaphoreType.REGULAR,
                 dma((groups - 1, chunks)), dma((groups - 1, chunks)), dma,
                 dma((groups - 1,)), dma((groups - 1,)), dma,
                 dma((groups - 1, chunks)), dma((groups - 1, chunks)), dma,
                 dma((peers,)), dma((peers,)),
+                dma((groups - 1,)), dma((groups - 1,)), dma,
+                dma((groups - 1,)), dma((groups - 1,)), dma, dma,
             ],
             compiler_params=pltpu.CompilerParams(
                 collective_id=0, has_side_effects=True, vmem_limit_bytes=56 * 2**20
             ),
         )(predicted_states, observed_truth, height_penalty_factor)
 
+
+        return pl.pallas_call(
+            functools.partial(settle, PIECES),
+            out_shape=(
+                jax.ShapeDtypeStruct(grad.shape, grad.dtype),
+                jax.ShapeDtypeStruct(loss.shape, loss.dtype),
+            ),
+            in_specs=[pl.BlockSpec(memory_space=pl.ANY)] * 2,
+            out_specs=(pl.BlockSpec(memory_space=pl.ANY),) * 2,
+            scratch_shapes=[dma((members, PIECES)), dma],
+        )(pltpu.with_memory_space_constraint(grad, pltpu.VMEM), pltpu.with_memory_space_constraint(loss, pltpu.VMEM))
+
     in_specs = (P("member", None, "band", None), P(None, "band", "member"), P())
     out_specs = (P("member", None, "band", None), P())
     return jax.shard_map(on_device, mesh=mesh, in_specs=in_specs, out_specs=out_specs, check_vma=False)

time: 64.8 us -> 60.1 us (0.927)
  Pallas kernels: 61.4 us -> 58.7 us
  local copies, waits for them, and re-layouts: 1.96 us -> 0 us
    pallas_call x1, Pallas kernels: 61.4 us -> 57.2 us  [on_device(): pl.pallas_call(functools.partial(kernel, sizes), out_shape=(pltpu.VMEM(pr...]
    unnamed x4 -> x0, local copies, waits for them, and re-layouts: 1.96 us -> none
    pallas_call x0 -> x1, Pallas kernels: none -> 1.48 us  [on_device(): pl.pallas_call(functools.partial(settle, PIECES), out_shape=(jax.ShapeDty...]
where the time goes in v3:
time: 60.1 us; the launch traced here: 59.3 us
  Pallas kernels  58.7 us (98%)
  between operations  0.64 us (1%)
    pallas_call x1, Pallas kernels, on_device(): pl.pallas_call(functools.partial(kernel, sizes), out_shape=(pltpu.VMEM(pr...  57.2 us
    pallas_call x1, Pallas kernels, on_device(): pl.pallas_call(functools.partial(settle, PIECES), out_shape=(jax.ShapeDty...  1.48 us

profile of v3, /device:TPU:1, one launch (start us, length us, event | category | flops | bytes accessed | tf_op | source)
XLA Modules:
  0.0 59.3 jit_solution(9091679306683812713)
XLA Ops:
  0.6 57.2 %shard_map.50 = (bf16[4,100,2,1440]{3,2,1,0:T(2,128)(2,1)S(1)}, f32[100]{0:T(128)S(1)}) custom-call(bf16[4,100,2,1440]{3,2,1,0:T(2,128)(2,1)} %x_ref.1, bf16[100,2,360]{2,1,0:T(2,128)(2,1)} %t_ref.1, f32[100]{0:T(128)} %w_hbm.1), custom_call_target="tpu_custom_call" | custom-call | tf_op jit(solution)/shard_map/pallas_call | solution.py:375
  57.8 1.5 %shard_map.51 = (bf16[4,100,2,1440]{3,2,1,0:T(2,128)(2,1)}, f32[100]{0:T(128)}) custom-call(bf16[4,100,2,1440]{3,2,1,0:T(2,128)(2,1)S(1)} %get-tuple-element.4.grad_ref, f32[100]{0:T(128)S(1)} %get-tuple-element.5.loss_ref), custom_call_target="tpu_custom_call" | custom-call | tf_op jit(solution)/shard_map/pallas_call | solution.py:412

commit v4 on v3

--- a/solution.py
+++ b/solution.py
@@ -14,7 +14,7 @@
 UP = 2.0**120
 STEP = 2.0**-13
 LANES = 128
-FRONT = 1024
+INNER = 2 * LANES
 PIECES = 1
 Z, CORES = 8, 2
 
@@ -49,16 +49,19 @@
 
 
 def kernel(
-    sizes, x_ref, t_ref, w_hbm, y_ref, loss_ref, xs, ts, tf, ys, area, part, ring, near, far, w_ref,
+    sizes, x_ref, t_ref, w_hbm, y_ref, loss_ref, xi, xo, ts, ti, tp, tq, to, yi, yo, area, part, ring, near, far, w_ref,
     x_edge, xe_out, xe_in, ye_out, ye_in, y_edge, ready, opened, *sems,
 ):
-    members, levels, rows, cells, groups, bands, chunks, early = sizes
-    own, deep = levels // groups, levels // groups // chunks
+    members, levels, rows, cells, groups, bands, chunks = sizes
+    own, deep = levels // groups, levels // chunks
     (x_send, x_recv, x_sem, t_send, t_recv, t_sem, y_send, y_recv, y_sem, l_send, l_recv) = sems[:11]
-    (xe_send, xe_recv, xe_sem, ye_send, ye_recv, ye_sem, w_sem) = sems[11:]
+    (xe_send, xe_recv, xe_sem, ye_send, ye_recv, ye_sem, w_sem) = sems[11:18]
+    (xo_send, xo_recv, xo_sem, yo_send, yo_recv, yo_sem, tq_sem) = sems[18:]
     whole = cells // LANES * LANES
     edge = cells - whole
-    body, rim = pl.ds(0, whole), pl.ds(whole, edge)
+    rim = pl.ds(whole, edge)
+    quarter, span = cells // groups, INNER + LANES
+    outers = whole // span
     everyone = groups * members
     me, band = lax.axis_index("member"), lax.axis_index("band")
     core, z, x = lax.rem(band, CORES), lax.rem(band // CORES, Z), band // (CORES * Z)
@@ -85,6 +88,8 @@
     keep_w.start()
     keep_xe = pltpu.make_async_copy(x_ref.at[:, :, :, rim], x_edge, xe_sem)
     keep_xe.start()
+    keep_t = pltpu.make_async_copy(t_ref, ts, t_sem)
+    keep_t.start()
     barrier = pltpu.get_barrier_semaphore()
 
     def greet(sem, peer):
@@ -118,24 +123,50 @@
         for peer in heads:
             greet(barrier, peer)
 
+    def peer_at(d):
+        return lax.rem(me + d, groups)
+
+    def deeps(c):
+        return pl.ds(deep * c, deep)
+
+    def paired(ref, d, c):
+        return ref.at[d, :, c // 2, :, :, pl.ds(pl.multiple_of(INNER * lax.rem(c, 2), LANES), INNER)]
+
+    def inside(q):
+        return pl.ds(pl.multiple_of(span * q, LANES), INNER)
+
+    def between(i):
+        return pl.ds(INNER + span * i, LANES)
+
+    def remote(src, dst, send, recv, d):
+        return pltpu.make_async_remote_copy(src, dst, send, recv, device_id=member_at(d), device_id_type=MESH)
+
     def send_t(d):
-        return pltpu.make_async_remote_copy(
-            t_ref.at[pl.ds(own * lax.rem(me + d, groups), own)], ts.at[me],
-            t_send.at[d - 1], t_recv.at[d - 1], device_id=member_at(d), device_id_type=MESH,
-        )
+        return remote(tp.at[pl.ds(own * peer_at(d), own)], tq.at[me], t_send.at[d - 1], t_recv.at[d - 1], d)
 
     def send_x(d, c):
-        return pltpu.make_async_remote_copy(
-            x_ref.at[:, pl.ds(own * lax.rem(me + d, groups) + deep * c, deep), :, body],
-            xs.at[groups - d, :, pl.ds(deep * c, deep)],
-            x_send.at[d - 1, c], x_recv.at[d - 1, c], device_id=member_at(d), device_id_type=MESH,
+        return remote(
+            x_ref.at[:, deeps(c), :, inside(peer_at(d))], paired(xi, groups - d, c),
+            x_send.at[d - 1, c], x_recv.at[d - 1, c], d,
+        )
+
+    def send_xo(d, i):
+        return remote(
+            x_ref.at[:, pl.ds(own * peer_at(d), own), :, between(i)],
+            xo.at[groups - d, :, :, :, pl.ds(LANES * i, LANES)],
+            xo_send.at[d - 1, i], xo_recv.at[d - 1, i], d,
         )
 
     def send_y(d, c):
-        return pltpu.make_async_remote_copy(
-            ys.at[d, :, pl.ds(deep * c, deep)],
-            y_ref.at[:, pl.ds(own * me + deep * c, deep), :, body],
-            y_send.at[d - 1, c], y_recv.at[d - 1, c], device_id=member_at(d), device_id_type=MESH,
+        return remote(
+            paired(yi, d, c), y_ref.at[:, deeps(c), :, inside(me)],
+            y_send.at[d - 1, c], y_recv.at[d - 1, c], d,
+        )
+
+    def send_yo(d, i):
+        return remote(
+            yo.at[d, :, :, :, pl.ds(LANES * i, LANES)], y_ref.at[:, pl.ds(own * me, own), :, between(i)],
+            yo_send.at[d - 1, i], yo_recv.at[d - 1, i], d,
         )
 
     def send_xe(d):
@@ -151,15 +182,46 @@
         )
 
     order = (1, 3, 2)
-    keep_t = pltpu.make_async_copy(t_ref.at[pl.ds(own * me, own)], ts.at[me], t_sem)
-    keep_x = pltpu.make_async_copy(x_ref.at[:, pl.ds(own * me, own), :, body], xs.at[0], x_sem)
+    keep_x = [
+        pltpu.make_async_copy(x_ref.at[:, deeps(c), :, inside(me)], paired(xi, 0, c), x_sem.at[c])
+        for c in range(chunks)
+    ]
+    keep_xo = [
+        pltpu.make_async_copy(
+            x_ref.at[:, pl.ds(own * me, own), :, between(i)],
+            xo.at[0, :, :, :, pl.ds(LANES * i, LANES)], xo_sem.at[i],
+        )
+        for i in range(outers)
+    ]
+    for c in range(2):
+        for d in order:
+            send_x(d, c).start()
+    for copy in keep_x + keep_xo:
+        copy.start()
+
+    keep_t.wait()
+    for q in range(groups):
+
+        @pl.when(me == q)
+        def _():
+            shift = (span - quarter) * q
+
+            def split(i, carry):
+                for c in range(chunks):
+                    row = ts[deep * c + i].astype(jnp.float32)
+                    ti[c // 2, i, :, pl.ds(INNER * (c % 2), INNER)] = row[:, shift : shift + INNER]
+                    rest = row[:, shift + INNER :]
+                    if shift:
+                        rest = jnp.concatenate([row[:, :shift], rest], axis=-1)
+                    tp[deep * c + i] = rest.astype(jnp.bfloat16)
+                return carry
+
+            lax.fori_loop(0, deep, split, 0)
+
     for d in order:
         send_t(d).start()
-    for c in range(early):
-        for d in order:
-            send_x(d, c).start()
-    keep_t.start()
-    keep_x.start()
+    keep_tq = pltpu.make_async_copy(tp.at[pl.ds(own * me, own)], tq.at[me], tq_sem)
+    keep_tq.start()
 
     keep_xe.wait()
 
@@ -182,7 +244,10 @@
     lax.fori_loop(0, everyone, pack, 0)
     for d in order:
         send_xe(d).start()
-    for c in range(early, chunks):
+    for i in range(outers):
+        for d in order:
+            send_xo(d, i).start()
+    for c in range(2, chunks):
         for d in order:
             send_x(d, c).start()
 
@@ -194,45 +259,66 @@
     lanes = lax.broadcasted_iota(jnp.int32, (8, 128), 1)
 
     keep_w.wait()
-    keep_t.wait()
-    keep_x.wait()
-    for d in order:
-        send_t(d).wait_recv()
-
-    def widen(v, carry):
-        tf[v] = jnp.concatenate([ts[p, v].astype(jnp.float32) for p in range(groups)], axis=-1)
+    for copy in keep_x + keep_xo:
+        copy.wait()
+    keep_tq.wait()
+
+    def level(ats, truth32, member_value, put):
+        width = truth32.shape[-1]
+        each = width // len(ats)
+        weights = [w_ref[at] for at in ats]
+        weight = weights[0]
+        if len(ats) > 1:
+            lane = lax.broadcasted_iota(jnp.int32, (rows, width), 1)
+            weight = jnp.where(lane < each, weights[0], weights[1])
+        area_here = area[:, pl.ds(0, width)]
+        block = rank_points(
+            [member_value(j) for j in range(everyone)],
+            truth32.astype(jnp.bfloat16), truth32, weight * area_here, member_value, put,
+        )
+        block = block * area_here
+        for i, at in enumerate(ats):
+            loss = jnp.sum(block[:, each * i : each * (i + 1)]) * weights[i] * (1.0 / (bands * rows * cells))
+            part[...] += jnp.where(lanes == at, loss, 0.0)
+
+    def inner_level(pair, i):
+        def member_value(j):
+            return xi[j // members, j % members, pair, i]
+
+        def put(j, value):
+            yi[j // members, j % members, pair, i] = value
+
+        level([2 * deep * pair + i, 2 * deep * pair + deep + i], ti[pair, i], member_value, put)
+
+    def outer_level(v, carry):
+        row = [tq[p, v].astype(jnp.float32) for p in range(groups)]
+        to[v] = jnp.concatenate(row, axis=-1)
+
+        def member_value(j):
+            return xo[j // members, j % members, v]
+
+        def put(j, value):
+            yo[j // members, j % members, v] = value
+
+        level([own * me + v], to[v, :, pl.ds(0, LANES * outers)], member_value, put)
         return carry
 
-    lax.fori_loop(0, own, widen, 0)
-
-    def level(v, carry):
-        weight = w_ref[own * me + v]
-        loss = None
-        for start, size in ((0, FRONT), (FRONT, whole - FRONT)):
-            cut = pl.ds(start, size)
-            truth32 = tf[v, :, cut]
-            area_here = area[:, cut]
-
-            def member_value(j):
-                return xs[j // members, j % members, v, :, cut]
-
-            def put(j, value):
-                ys[j // members, j % members, v, :, cut] = value
-
-            block = rank_points(
-                [member_value(j) for j in range(everyone)],
-                truth32.astype(jnp.bfloat16), truth32, weight * area_here, member_value, put,
-            )
-            block = jnp.sum(block * area_here)
-            loss = block if loss is None else loss + block
-        loss = loss * weight * (1.0 / (bands * rows * cells))
-        part[...] += jnp.where(lanes == own * me + v, loss, 0.0)
-        return carry
+    def outside():
+        for d in order:
+            send_t(d).wait_recv()
+        for i in range(outers):
+            for d in order:
+                send_xo(d, i).wait_recv()
+        lax.fori_loop(0, own, outer_level, 0)
+        for i in range(outers):
+            for d in order:
+                send_yo(d, i).start()
+        edges()
 
     def edges():
         for d in order:
             send_xe(d).wait_recv()
-        truth32 = jnp.concatenate([tf[v, :, rim] for v in range(own)], axis=-1)
+        truth32 = jnp.concatenate([to[v, :, pl.ds(LANES * outers, edge)] for v in range(own)], axis=-1)
         weights = [w_ref[own * me + v] for v in range(own)]
         area_here = area[:, : own * edge]
         wide_weight = jnp.concatenate([jnp.full((rows, edge), w, jnp.float32) for w in weights], axis=-1)
@@ -258,8 +344,32 @@
         for d in order:
             send_ye(d).start()
 
-    def chunk(c, carry):
-        @pl.when(head & (c == 2))
+    def move(src, dst, i, peer):
+        return pltpu.make_async_remote_copy(
+            src, dst, l_send.at[i], l_recv.at[i], device_id=peer, device_id_type=MESH
+        )
+
+    def add_up(slots, count):
+        total = slots[0]
+        for i in range(1, count):
+            total = total + slots[i]
+        return total
+
+    def hand_out(slots, count, mine, at, base):
+        slots[mine] = part[...]
+        for d in range(1, count):
+            move(part, slots.at[mine], base + d - 1, at(d)).start()
+
+    def take_in(slots, count, mine, at, base):
+        for d in range(1, count):
+            move(part, slots.at[mine], base + d - 1, at(d)).wait()
+        part[...] = add_up(slots, count)
+
+    by_x = (near, wide * CORES, x * CORES + core, around, 0)
+    by_z = (far, tall, z, along, wide * CORES)
+    by_y = (ring, groups, me, member_at, wide * CORES + tall)
+    def chunk_pair(pair, carry):
+        @pl.when(head & (pair == 1))
         def _():
             pl.semaphore_wait(barrier, len(heads))
             for m in range(groups):
@@ -267,47 +377,44 @@
                     if m + other:
                         greet(opened, {"member": m, "band": band + other})
 
-        for d in order:
-            send_x(d, c).wait_recv()
-        lax.fori_loop(c * deep, (c + 1) * deep, level, 0)
-        for d in order:
-            send_y(d, c).start()
-        pl.when(c == early - 1)(edges)
+        for half in range(2):
+            for d in order:
+                send_x(d, 2 * pair + half).wait_recv()
+
+        def step(i, carry):
+            inner_level(pair, i)
+            return carry
+
+        lax.fori_loop(0, deep, step, 0)
+        @pl.when(pair == chunks // 2 - 1)
+        def _():
+            @pl.when(jnp.logical_not(head))
+            def _():
+                pl.semaphore_wait(opened, 1)
+
+            hand_out(*by_x)
+
+        for half in range(2):
+            for d in order:
+                send_y(d, 2 * pair + half).start()
+        pl.when(pair == 0)(outside)
         return carry
 
-    lax.fori_loop(0, chunks, chunk, 0)
-    keep_y = pltpu.make_async_copy(ys.at[0], y_ref.at[:, pl.ds(own * me, own), :, body], y_sem)
-    keep_y.start()
-
-    def move(src, dst, i, peer):
-        return pltpu.make_async_remote_copy(
-            src, dst, l_send.at[i], l_recv.at[i], device_id=peer, device_id_type=MESH
-        )
-
-    def add_up(slots, count):
-        total = slots[0]
-        for i in range(1, count):
-            total = total + slots[i]
-        return total
-
-    def hand_out(slots, count, mine, at, base):
-        slots[mine] = part[...]
-        for d in range(1, count):
-            move(part, slots.at[mine], base + d - 1, at(d)).start()
-
-    def take_in(slots, count, mine, at, base):
-        for d in range(1, count):
-            move(part, slots.at[mine], base + d - 1, at(d)).wait()
-        part[...] = add_up(slots, count)
-
-    @pl.when(jnp.logical_not(head))
-    def _():
-        pl.semaphore_wait(opened, 1)
-
-    by_x = (near, wide * CORES, x * CORES + core, around, 0)
-    by_z = (far, tall, z, along, wide * CORES)
-    by_y = (ring, groups, me, member_at, wide * CORES + tall)
-    hand_out(*by_x)
+    lax.fori_loop(0, chunks // 2, chunk_pair, 0)
+    keep_y = [
+        pltpu.make_async_copy(paired(yi, 0, c), y_ref.at[:, deeps(c), :, inside(me)], y_sem.at[c])
+        for c in range(chunks)
+    ]
+    keep_y += [
+        pltpu.make_async_copy(
+            yo.at[0, :, :, :, pl.ds(LANES * i, LANES)],
+            y_ref.at[:, pl.ds(own * me, own), :, between(i)], yo_sem.at[i],
+        )
+        for i in range(outers)
+    ]
+    for copy in keep_y:
+        copy.start()
+
     take_in(*by_x)
     hand_out(*by_z)
     take_in(*by_z)
@@ -326,13 +433,13 @@
     lax.fori_loop(0, everyone, unpack, 0)
     keep_ye = pltpu.make_async_copy(y_edge, y_ref.at[:, :, :, rim], ye_sem)
     keep_ye.start()
-    take_in(*by_y)
-    loss_ref[...] = part[0, :levels]
-
     for d in order:
         send_t(d).wait_send()
         send_xe(d).wait_send()
         send_ye(d).wait_send()
+        for i in range(outers):
+            send_xo(d, i).wait_send()
+            send_yo(d, i).wait()
 
     def drain(c, carry):
         for d in order:
@@ -341,8 +448,11 @@
         return carry
 
     lax.fori_loop(0, chunks, drain, 0)
-    keep_y.wait()
+    for copy in keep_y:
+        copy.wait()
     keep_ye.wait()
+    take_in(*by_y)
+    loss_ref[...] = part[0, :levels]
 
 
 def settle(pieces, grad_ref, loss_ref, grad_out, loss_out, sems, loss_sem):
@@ -361,13 +471,17 @@
 
 def solution(mesh):
     groups, bands = mesh.shape["member"], mesh.shape["band"]
-    chunks, early = 5, 2
+    chunks = 4
 
     def on_device(predicted_states, observed_truth, height_penalty_factor):
         members, levels, rows, cells = predicted_states.shape
         own = levels // groups
-        sizes = (members, levels, rows, cells, groups, bands, chunks, early)
+        sizes = (members, levels, rows, cells, groups, bands, chunks)
         whole = cells // LANES * LANES
+        quarter, outers = cells // groups, whole // (INNER + LANES)
+        deep = levels // chunks
+        inner = (groups, members, chunks // 2, deep, rows, 2 * INNER)
+        outer = (groups, members, own, rows, outers * LANES)
         packed = (groups, members, rows, own * (cells - whole))
         wide, tall = bands // (CORES * Z), Z
         dma = pltpu.SemaphoreType.DMA
@@ -381,10 +495,15 @@
             in_specs=[pl.BlockSpec(memory_space=pltpu.HBM)] * 2 + [pl.BlockSpec(memory_space=pltpu.HBM)],
             out_specs=(pl.BlockSpec(memory_space=pl.ANY), pl.BlockSpec(memory_space=pltpu.VMEM)),
             scratch_shapes=[
-                pltpu.VMEM((groups, members, own, rows, whole), jnp.bfloat16),
-                pltpu.VMEM((groups, own, rows, cells // groups), jnp.bfloat16),
-                pltpu.VMEM((own, rows, cells), jnp.float32),
-                pltpu.VMEM((groups, members, own, rows, whole), jnp.bfloat16),
+                pltpu.VMEM(inner, jnp.bfloat16),
+                pltpu.VMEM(outer, jnp.bfloat16),
+                pltpu.VMEM((levels, rows, quarter), jnp.bfloat16),
+                pltpu.VMEM((chunks // 2, deep, rows, 2 * INNER), jnp.float32),
+                pltpu.VMEM((levels, rows, quarter - INNER), jnp.bfloat16),
+                pltpu.VMEM((groups, own, rows, quarter - INNER), jnp.bfloat16),
+                pltpu.VMEM((own, rows, groups * (quarter - INNER)), jnp.float32),
+                pltpu.VMEM(inner, jnp.bfloat16),
+                pltpu.VMEM(outer, jnp.bfloat16),
                 pltpu.VMEM((rows, cells), jnp.float32),
                 pltpu.VMEM((8, 128), jnp.float32),
                 pltpu.VMEM((groups, 8, 128), jnp.float32),
@@ -396,12 +515,14 @@
                 pltpu.VMEM(packed, jnp.bfloat16), pltpu.VMEM(packed, jnp.bfloat16),
                 pltpu.VMEM((members, levels, rows, cells - whole), jnp.bfloat16),
                 pltpu.SemaphoreType.REGULAR, pltpu.SemaphoreType.REGULAR,
-                dma((groups - 1, chunks)), dma((groups - 1, chunks)), dma,
+                dma((groups - 1, chunks)), dma((groups - 1, chunks)), dma((chunks,)),
                 dma((groups - 1,)), dma((groups - 1,)), dma,
-                dma((groups - 1, chunks)), dma((groups - 1, chunks)), dma,
+                dma((groups - 1, chunks)), dma((groups - 1, chunks)), dma((chunks,)),
                 dma((peers,)), dma((peers,)),
                 dma((groups - 1,)), dma((groups - 1,)), dma,
                 dma((groups - 1,)), dma((groups - 1,)), dma, dma,
+                dma((groups - 1, outers)), dma((groups - 1, outers)), dma((outers,)),
+                dma((groups - 1, outers)), dma((groups - 1, outers)), dma((outers,)), dma,
             ],
             compiler_params=pltpu.CompilerParams(
                 collective_id=0, has_side_effects=True, vmem_limit_bytes=56 * 2**20

time: 60.1 us -> 60 us (level); the launches traced: 59.3 us -> 59.9 us
  no operation moved by 1% of the time
where the time goes in v4:
time: 60 us; the launch traced here: 59.9 us
  Pallas kernels  59.2 us (99%)
  between operations  0.64 us (1%)
    pallas_call x1, Pallas kernels, on_device(): pl.pallas_call(functools.partial(kernel, sizes), out_shape=(pltpu.VMEM(pr...  57.7 us
    pallas_call x1, Pallas kernels, on_device(): pl.pallas_call(functools.partial(settle, PIECES), out_shape=(jax.ShapeDty...  1.48 us

profile of v4, /device:TPU:1, one launch (start us, length us, event | category | flops | bytes accessed | tf_op | source)
XLA Modules:
  0.0 59.9 jit_solution(10862017410538791610)
XLA Ops:
  0.6 57.7 %shard_map.50 = (bf16[4,100,2,1440]{3,2,1,0:T(2,128)(2,1)S(1)}, f32[100]{0:T(128)S(1)}) custom-call(bf16[4,100,2,1440]{3,2,1,0:T(2,128)(2,1)} %x_ref.1, bf16[100,2,360]{2,1,0:T(2,128)(2,1)} %t_ref.1, f32[100]{0:T(128)} %w_hbm.1), custom_call_target="tpu_custom_call" | custom-call | tf_op jit(solution)/shard_map/pallas_call | solution.py:489
  58.4 1.5 %shard_map.51 = (bf16[4,100,2,1440]{3,2,1,0:T(2,128)(2,1)}, f32[100]{0:T(128)}) custom-call(bf16[4,100,2,1440]{3,2,1,0:T(2,128)(2,1)S(1)} %get-tuple-element.4.grad_ref, f32[100]{0:T(128)S(1)} %get-tuple-element.5.loss_ref), custom_call_target="tpu_custom_call" | custom-call | tf_op jit(solution)/shard_map/pallas_call | solution.py:533

commit v5 on v4

--- a/solution.py
+++ b/solution.py
@@ -385,7 +385,7 @@
             inner_level(pair, i)
             return carry
 
-        lax.fori_loop(0, deep, step, 0)
+        lax.fori_loop(0, deep, step, 0, unroll=5)
         @pl.when(pair == chunks // 2 - 1)
         def _():
             @pl.when(jnp.logical_not(head))

time: 60 us -> 59.2 us (0.987)
  Pallas kernels: 59.2 us -> 57.8 us
    pallas_call x1, Pallas kernels: 57.7 us -> 56.4 us  [on_device(): pl.pallas_call(functools.partial(kernel, sizes), out_shape=(pltpu.VMEM(pr...]
where the time goes in v5:
time: 59.2 us; the launch traced here: 58.5 us
  Pallas kernels  57.8 us (98%)
  between operations  0.64 us (1%)
    pallas_call x1, Pallas kernels, on_device(): pl.pallas_call(functools.partial(kernel, sizes), out_shape=(pltpu.VMEM(pr...  56.4 us
    pallas_call x1, Pallas kernels, on_device(): pl.pallas_call(functools.partial(settle, PIECES), out_shape=(jax.ShapeDty...  1.48 us

profile of v5, /device:TPU:1, one launch (start us, length us, event | category | flops | bytes accessed | tf_op | source)
XLA Modules:
  0.0 58.5 jit_solution(2902279846844719935)
XLA Ops:
  0.6 56.4 %shard_map.50 = (bf16[4,100,2,1440]{3,2,1,0:T(2,128)(2,1)S(1)}, f32[100]{0:T(128)S(1)}) custom-call(bf16[4,100,2,1440]{3,2,1,0:T(2,128)(2,1)} %x_ref.1, bf16[100,2,360]{2,1,0:T(2,128)(2,1)} %t_ref.1, f32[100]{0:T(128)} %w_hbm.1), custom_call_target="tpu_custom_call" | custom-call | tf_op jit(solution)/shard_map/pallas_call | solution.py:489
  57.0 1.5 %shard_map.51 = (bf16[4,100,2,1440]{3,2,1,0:T(2,128)(2,1)}, f32[100]{0:T(128)}) custom-call(bf16[4,100,2,1440]{3,2,1,0:T(2,128)(2,1)S(1)} %get-tuple-element.4.grad_ref, f32[100]{0:T(128)S(1)} %get-tuple-element.5.loss_ref), custom_call_target="tpu_custom_call" | custom-call | tf_op jit(solution)/shard_map/pallas_call | solution.py:533
